TPU v7x, 32 devices: a whole 2x2x4 slice. The times are simulated.
32 devices in a mesh: dp: 4 (over y, x), seq: 8 (over z, core).
Axes of the slice: x: 2, y: 2, z: 4, core: 2. Of those that a mesh axis runs over, the one named last changes fastest.
Arguments:
- inputs: bfloat16 [2, 4, 2048, 768], P(None, 'dp', 'seq'), may hold values from -6 to 6
- offsets: int32 [2, 4, 2048], P(None, 'dp', 'seq'), may hold values from 0 to 2045, as said below
- w_query: bfloat16 [768, 768], P(('dp', 'seq')), may hold values from -0.21875 to 0.21875
- w_kv: bfloat16 [768, 128], P(('dp', 'seq')), may hold values from -0.21875 to 0.21875
- w_out: bfloat16 [768, 768], P(('dp', 'seq')), may hold values from -0.875 to 0.875
- w_up: bfloat16 [768, 3072], P(('dp', 'seq')), may hold values from -0.21875 to 0.21875
- w_down: bfloat16 [3072, 768], P(('dp', 'seq')), may hold values from -0.109375 to 0.109375
- b_up: bfloat16 [3072], P(('dp', 'seq')), may hold values from -1.5 to 1.5
- vectors: bfloat16 [7, 768], P(None, ('dp', 'seq')), may hold values from -1.5 to 1.5
- b_kv: bfloat16 [128], replicated, may hold values from -2.5 to 2.5
- cotangent: bfloat16 [2, 4, 2048, 768], P(None, 'dp', 'seq'), may hold values from -6 to 6
Outputs:
- out: bfloat16 [2, 4, 2048, 768], P(None, 'dp', 'seq')
- grad_inputs: float32 [2, 4, 2048, 768], P(None, 'dp', 'seq')
- grad_w_query: float32 [768, 768], P(('dp', 'seq'))
- grad_w_kv: float32 [768, 128], P(('dp', 'seq'))
- grad_w_out: float32 [768, 768], P(('dp', 'seq'))
- grad_w_up: float32 [768, 3072], P(('dp', 'seq'))
- grad_w_down: float32 [3072, 768], P(('dp', 'seq'))
- grad_b_up: float32 [3072], P(('dp', 'seq'))
- grad_vectors: float32 [7, 768], P(None, ('dp', 'seq'))
- grad_b_kv: float32 [128], replicated
Inputs may be any that keep to these rules, and one draw needn't show every extreme that they name: Each sequence holds three documents end to end; offsets count 0, 1, 2, ... within each document; the first and the last document have 1 to 128 positions, and in some sequence of every draw both have exactly one.
All inputs are finite; a program needn't handle non-finite values.
Results may differ from a plain program's by a relative error of at most 0.011.
Values may be sent and summed in bfloat16 or wider, within the bound.
A program may use at most 128 MiB of HBM per device.

v0:
```python
import math

import jax
import jax.numpy as jnp
from jax import lax
from jax.sharding import PartitionSpec as P

H = 12
HD = 64
ROT = 16


epsilon = 1e-05
root_half = 0.7071067811865476
density_scale = 0.3989422804014327
masked_score = -1e30


def normalize(values):
    average = jnp.mean(values, axis=-1, keepdims=True)
    centered = values - average
    inverse = lax.rsqrt(jnp.mean(centered * centered, axis=-1, keepdims=True) + epsilon)
    return (centered * inverse, inverse)


def norm_back(grad_out, normed, inverse, gain_row):
    scaled = grad_out * gain_row
    first_mean = jnp.mean(scaled, axis=-1, keepdims=True)
    second_mean = jnp.mean(scaled * normed, axis=-1, keepdims=True)
    return inverse * (scaled - first_mean - normed * second_mean)


def rotate(values, cosine, sine_part):
    half_rot = ROT // 2
    first_part = values[..., :half_rot]
    second = values[..., half_rot:ROT]
    return jnp.concatenate(
        [
            first_part * cosine - second * sine_part,
            second * cosine + first_part * sine_part,
            values[..., ROT:],
        ],
        axis=-1,
    )


def gelu_slope(hidden):
    return 0.5 * (1.0 + lax.erf(hidden * root_half)) + hidden * density_scale * jnp.exp(
        -0.5 * hidden * hidden
    )


def tree_add(left_tree, right_tree):
    return tuple((left_item + right_item for left_item, right_item in zip(left_tree, right_tree)))


def on_device(inputs, offsets, w_query, w_kv, w_out, w_up, w_down, b_up, vectors, b_kv, cotangent):
    micro_count = inputs.shape[0]
    local_rows = inputs.shape[2]
    model_width = inputs.shape[3]
    seqlen = local_rows * lax.axis_size("seq")
    key_block = math.gcd(seqlen, 512)
    first_row = lax.axis_index("seq") * local_rows
    blocks_used = (first_row + local_rows + key_block - 1) // key_block
    row_ids = first_row + jnp.arange(local_rows, dtype=jnp.int32)
    half_rot = ROT // 2
    frequency = jnp.power(10000.0, -jnp.arange(half_rot, dtype=jnp.float32) * (2.0 / ROT))
    kv_bias = b_kv.astype(jnp.float32)
    results = []
    input_grads = []
    totals = None
    kv_bias_total = jnp.zeros(b_kv.shape, jnp.float32)
    for micro_index in range(micro_count):
        values_in = inputs[micro_index, 0].astype(jnp.float32)
        row_offsets = offsets[micro_index, 0]
        upstream = cotangent[micro_index, 0]
        upstream_f = upstream.astype(jnp.float32)
        angle = (row_offsets.astype(jnp.float32) * 0.25)[:, None] * frequency[None, :]
        cosine = jnp.cos(angle)
        sine_part = jnp.sin(angle)
        gathered = (
            lax.all_gather(w_query, ("dp", "seq"), axis=0, tiled=True),
            lax.all_gather(w_kv, ("dp", "seq"), axis=0, tiled=True),
            lax.all_gather(w_out, ("dp", "seq"), axis=0, tiled=True),
            lax.all_gather(w_up, ("dp", "seq"), axis=0, tiled=True),
            lax.all_gather(w_down, ("dp", "seq"), axis=0, tiled=True),
            lax.all_gather(b_up, ("dp", "seq"), axis=0, tiled=True),
            lax.all_gather(vectors, ("dp", "seq"), axis=1, tiled=True),
        )
        query_full, kv_full, out_full, up_full, down_full, up_bias, vector_full = gathered
        vector_f = vector_full.astype(jnp.float32)
        normed1, inverse1 = normalize(values_in)
        hidden1 = (normed1 * vector_f[0] + vector_f[1]).astype(jnp.bfloat16)
        query_pre = jnp.dot(hidden1, query_full, preferred_element_type=jnp.float32) + vector_f[4]
        kv_pre = jnp.dot(hidden1, kv_full, preferred_element_type=jnp.float32) + kv_bias
        queries = rotate(
            query_pre.reshape(local_rows, H, HD), cosine[:, None, :], sine_part[:, None, :]
        ).astype(jnp.bfloat16)
        shared_local = jnp.concatenate(
            [rotate(kv_pre[:, :HD], cosine, sine_part), kv_pre[:, HD:]], axis=1
        ).astype(jnp.bfloat16)
        shared = lax.all_gather(shared_local, "seq", axis=0, tiled=True)

        def block_scores(number):
            start_row = number * key_block
            key_piece = lax.dynamic_slice_in_dim(shared, start_row, key_block, 0)
            columns = start_row + jnp.arange(key_block, dtype=jnp.int32)
            allowed = (columns[None, :] <= row_ids[:, None]) & (
                row_ids[:, None] - columns[None, :] <= row_offsets[:, None]
            )
            scores = (
                jnp.einsum(
                    "rhd,kd->hrk", queries, key_piece[:, :HD], preferred_element_type=jnp.float32
                )
                * 0.125
            )
            return (jnp.where(allowed[None], scores, masked_score), key_piece)

        def max_step(number, state_pair):
            running_top, denominator = state_pair
            scores, key_piece = block_scores(number)
            new_top = jnp.maximum(running_top, jnp.max(scores, axis=-1))
            denominator = denominator * jnp.exp(running_top - new_top) + jnp.sum(
                jnp.exp(scores - new_top[..., None]), axis=-1
            )
            return (new_top, denominator)

        start_top = jnp.full((H, local_rows), masked_score, jnp.float32)
        running_top, denominator = lax.fori_loop(
            0, blocks_used, max_step, (start_top, jnp.zeros((H, local_rows), jnp.float32))
        )
        log_total = running_top + jnp.log(denominator)

        def value_step(number, accumulated):
            scores, key_piece = block_scores(number)
            soft_weights = jnp.exp(scores - log_total[..., None]).astype(jnp.bfloat16)
            return accumulated + jnp.einsum(
                "hrk,kd->rhd", soft_weights, key_piece[:, HD:], preferred_element_type=jnp.float32
            )

        attended_f = lax.fori_loop(
            0, blocks_used, value_step, jnp.zeros((local_rows, H, HD), jnp.float32)
        )
        attended = attended_f.reshape(local_rows, model_width).astype(jnp.bfloat16)
        attn_out = jnp.dot(attended, out_full, preferred_element_type=jnp.float32) + vector_f[5]
        normed2, inverse2 = normalize(values_in)
        hidden2 = (normed2 * vector_f[2] + vector_f[3]).astype(jnp.bfloat16)
        hidden_up = jnp.dot(hidden2, up_full, preferred_element_type=jnp.float32) + up_bias.astype(
            jnp.float32
        )
        activated = jax.nn.gelu(hidden_up, approximate=False).astype(jnp.bfloat16)
        mlp_out = jnp.dot(activated, down_full, preferred_element_type=jnp.float32) + vector_f[6]
        results.append((values_in + attn_out + mlp_out).astype(jnp.bfloat16))
        regathered = (
            lax.all_gather(w_query, ("dp", "seq"), axis=0, tiled=True),
            lax.all_gather(w_kv, ("dp", "seq"), axis=0, tiled=True),
            lax.all_gather(w_out, ("dp", "seq"), axis=0, tiled=True),
            lax.all_gather(w_up, ("dp", "seq"), axis=0, tiled=True),
            lax.all_gather(w_down, ("dp", "seq"), axis=0, tiled=True),
            lax.all_gather(b_up, ("dp", "seq"), axis=0, tiled=True),
            lax.all_gather(vectors, ("dp", "seq"), axis=1, tiled=True),
        )
        query_back, kv_back, out_back, up_back, down_back, up_bias_back, vector_back = regathered
        vector_back_f = vector_back.astype(jnp.float32)
        grad_w_down = jnp.einsum(
            "rf,rd->fd", activated, upstream, preferred_element_type=jnp.float32
        )
        d_act = jnp.einsum("rd,fd->rf", upstream, down_back, preferred_element_type=jnp.float32)
        d_hidden = (d_act * gelu_slope(hidden_up)).astype(jnp.bfloat16)
        grad_w_up = jnp.einsum("rd,rf->df", hidden2, d_hidden, preferred_element_type=jnp.float32)
        grad_b_up = jnp.sum(d_hidden.astype(jnp.float32), axis=0)
        d_normed2 = jnp.einsum("rf,df->rd", d_hidden, up_back, preferred_element_type=jnp.float32)
        grad_w_out = jnp.einsum("rd,re->de", attended, upstream, preferred_element_type=jnp.float32)
        d_attended = (
            jnp.einsum("re,de->rd", upstream, out_back, preferred_element_type=jnp.float32)
            .astype(jnp.bfloat16)
            .reshape(local_rows, H, HD)
        )

        def delta_step(number, accumulated):
            scores, key_piece = block_scores(number)
            soft_probs = jnp.exp(scores - log_total[..., None])
            d_probs = jnp.einsum(
                "rhd,kd->hrk", d_attended, key_piece[:, HD:], preferred_element_type=jnp.float32
            )
            return accumulated + jnp.sum(soft_probs * d_probs, axis=-1)

        delta = lax.fori_loop(0, blocks_used, delta_step, jnp.zeros((H, local_rows), jnp.float32))

        def grad_step(number, state_pair):
            d_query_rot, d_shared_all = state_pair
            start_row = number * key_block
            scores, key_piece = block_scores(number)
            soft_probs = jnp.exp(scores - log_total[..., None])
            d_probs = jnp.einsum(
                "rhd,kd->hrk", d_attended, key_piece[:, HD:], preferred_element_type=jnp.float32
            )
            d_scores = (soft_probs * (d_probs - delta[..., None])).astype(jnp.bfloat16)
            d_query_rot = (
                d_query_rot
                + jnp.einsum(
                    "hrk,kd->rhd", d_scores, key_piece[:, :HD], preferred_element_type=jnp.float32
                )
                * 0.125
            )
            d_keys = (
                jnp.einsum("hrk,rhd->kd", d_scores, queries, preferred_element_type=jnp.float32)
                * 0.125
            )
            d_values = jnp.einsum(
                "hrk,rhd->kd",
                soft_probs.astype(jnp.bfloat16),
                d_attended,
                preferred_element_type=jnp.float32,
            )
            current = lax.dynamic_slice_in_dim(d_shared_all, start_row, key_block, 0)
            d_shared_all = lax.dynamic_update_slice_in_dim(
                d_shared_all, current + jnp.concatenate([d_keys, d_values], axis=1), start_row, 0
            )
            return (d_query_rot, d_shared_all)

        d_query_rot, d_shared_all = lax.fori_loop(
            0,
            blocks_used,
            grad_step,
            (jnp.zeros((local_rows, H, HD), jnp.float32), jnp.zeros((seqlen, 2 * HD), jnp.float32)),
        )
        d_shared_mine = lax.psum_scatter(
            d_shared_all.astype(jnp.bfloat16), "seq", scatter_dimension=0, tiled=True
        ).astype(jnp.float32)
        d_shared = jnp.concatenate(
            [rotate(d_shared_mine[:, :HD], cosine, -sine_part), d_shared_mine[:, HD:]], axis=1
        ).astype(jnp.bfloat16)
        d_queries = (
            rotate(d_query_rot, cosine[:, None, :], -sine_part[:, None, :])
            .reshape(local_rows, model_width)
            .astype(jnp.bfloat16)
        )
        grad_w_query = jnp.einsum(
            "rd,re->de", hidden1, d_queries, preferred_element_type=jnp.float32
        )
        grad_w_kv = jnp.einsum("rd,rc->dc", hidden1, d_shared, preferred_element_type=jnp.float32)
        kv_bias_total = kv_bias_total + jnp.sum(d_shared.astype(jnp.float32), axis=0)
        d_normed1 = jnp.einsum(
            "re,de->rd", d_queries, query_back, preferred_element_type=jnp.float32
        ) + jnp.einsum("rc,dc->rd", d_shared, kv_back, preferred_element_type=jnp.float32)
        upstream_sum = jnp.sum(upstream_f, axis=0)
        grad_vectors = jnp.stack(
            [
                jnp.sum(d_normed1 * normed1, axis=0),
                jnp.sum(d_normed1, axis=0),
                jnp.sum(d_normed2 * normed2, axis=0),
                jnp.sum(d_normed2, axis=0),
                jnp.sum(d_queries.astype(jnp.float32), axis=0),
                upstream_sum,
                upstream_sum,
            ]
        )
        input_grads.append(
            upstream_f
            + norm_back(d_normed1, normed1, inverse1, vector_back_f[0])
            + norm_back(d_normed2, normed2, inverse2, vector_back_f[2])
        )
        shares = (
            lax.psum_scatter(grad_w_query, ("dp", "seq"), scatter_dimension=0, tiled=True),
            lax.psum_scatter(grad_w_kv, ("dp", "seq"), scatter_dimension=0, tiled=True),
            lax.psum_scatter(grad_w_out, ("dp", "seq"), scatter_dimension=0, tiled=True),
            lax.psum_scatter(grad_w_up, ("dp", "seq"), scatter_dimension=0, tiled=True),
            lax.psum_scatter(grad_w_down, ("dp", "seq"), scatter_dimension=0, tiled=True),
            lax.psum_scatter(grad_b_up, ("dp", "seq"), scatter_dimension=0, tiled=True),
            lax.psum_scatter(grad_vectors, ("dp", "seq"), scatter_dimension=1, tiled=True),
        )
        totals = shares if totals is None else tree_add(totals, shares)
    kv_bias_grad = lax.psum(kv_bias_total, ("dp", "seq"))
    return (
        jnp.stack(results)[:, None],
        jnp.stack(input_grads)[:, None],
        totals[0],
        totals[1],
        totals[2],
        totals[3],
        totals[4],
        totals[5],
        totals[6],
        kv_bias_grad,
    )


def solution(mesh):
    in_specs = (
        P(None, "dp", "seq", None),
        P(None, "dp", "seq"),
        P(("dp", "seq"), None),
        P(("dp", "seq"), None),
        P(("dp", "seq"), None),
        P(("dp", "seq"), None),
        P(("dp", "seq"), None),
        P(("dp", "seq")),
        P(None, ("dp", "seq")),
        P(),
        P(None, "dp", "seq", None),
    )
    out_specs = (
        P(None, "dp", "seq", None),
        P(None, "dp", "seq", None),
        P(("dp", "seq"), None),
        P(("dp", "seq"), None),
        P(("dp", "seq"), None),
        P(("dp", "seq"), None),
        P(("dp", "seq"), None),
        P(("dp", "seq")),
        P(None, ("dp", "seq")),
        P(),
    )
    return jax.shard_map(
        on_device, mesh=mesh, in_specs=in_specs, out_specs=out_specs, check_vma=False
    )
```

profile of v0, /device:TPU:0, one launch (start us, length us, event | category | flops | bytes accessed | tf_op | source)
XLA Modules:
  0.0 1150.0 jit_solution(11394864214349729968)
XLA Ops:
  13.5 43.7 %all-gather = bf16[32,24,7]{1,2,0:T(8,128)(2,1)S(1)} all-gather(bf16[1,24,7]{1,2,0:T(8,128)(2,1)} %bitcast.605), channel_id=1, replica_groups=mesh['dp'=4,'seq'=8] {'dp','seq'}, dimensions={0}, use_global_device_ids=true | all-gather | bytes 11088 | tf_op jit(solution)/shard_map/all_gather | solution.py:88
  58.2 37.7 %all_gather.19 = bf16[768,128]{1,0:T(8,128)(2,1)S(1)} all-gather(bf16[24,128]{1,0:T(8,128)(2,1)} %param.30), channel_id=1, replica_groups=mesh['dp'=4,'seq'=8] {'dp','seq'}, dimensions={0}, use_global_device_ids=true | all-gather | bytes 202752 | tf_op jit(solution)/shard_map/all_gather | solution.py:83
  98.1 15.0 %all_gather.20 = bf16[2048,128]{0,1:T(8,128)(2,1)S(1)} all-gather(bf16[256,128]{0,1:T(8,128)(2,1)S(1)} %pad_maximum_fusion.2), channel_id=1, replica_groups=mesh['dp'=4,'seq'=8] {'seq'}, dimensions={0}, use_global_device_ids=true | all-gather | bytes 589824 | tf_op jit(solution)/shard_map/all_gather | solution.py:102
  128.0 8.6 while.100
  131.9 4.6 fusion.417
  138.6 16.1 %while.101 = (s32[]{:T(128)}, f32[256,12,64]{0,2,1:T(8,128)S(1)}, f32[2048,128]{0,1:T(8,128)}, s32[]{:T(128)}, bf16[2048,128]{0,1:T(8,128)(2,1)}, /*index=5*/s32...) while((s32[]{:T(128)}, f32[256,12,64]{0,2,1:T(8,128)S(1)}, ...), condition=%wide.region_20.21_spmd.clone, body=%wide.region_19.20_spmd.clone.sunk | while | flops 1023443712 | bytes 59878692 | solution.py:222
  139.2 4.5 fusion.425
  143.9 5.0 fusion.427
  166.3 96.1 %reduce-scatter.11.cloned.1.call-done = bf16[256,128]{0,1:T(8,128)(2,1)} async-done(((bf16[2048,128]{0,1:T(8,128)(2,1)}), bf16[256,128]{0,1:T(8,128)(2,1)}) %reduce-scatter.11.cloned.1.call-update) | async-done | bytes 65552 | tf_op jit(solution)/shard_map/reduce_scatter | solution.py:228
  264.2 15.0 %all_gather.26 = bf16[2048,128]{0,1:T(8,128)(2,1)S(1)} all-gather(bf16[256,128]{0,1:T(8,128)(2,1)S(1)} %pad_maximum_fusion.3), channel_id=1, replica_groups=mesh['dp'=4,'seq'=8] {'seq'}, dimensions={0}, use_global_device_ids=true | all-gather | bytes 589824 | tf_op jit(solution)/shard_map/all_gather | solution.py:102
  283.0 8.9 while.102
  287.0 4.8 fusion.436
  293.8 15.6 %while.103 = (s32[]{:T(128)}, f32[256,12,64]{0,2,1:T(8,128)S(1)}, f32[2048,128]{0,1:T(8,128)}, s32[]{:T(128)}, bf16[2048,128]{0,1:T(8,128)(2,1)}, /*index=5*/s32...) while((s32[]{:T(128)}, f32[256,12,64]{0,2,1:T(8,128)S(1)}, ...), condition=%wide.region_30.31_spmd.clone, body=%wide.region_29.30_spmd.clone.sunk | while | flops 1023443712 | bytes 59878692 | solution.py:222
  293.8 4.5 fusion.444
  298.5 5.0 fusion.446
  313.8 4.3 while.97
  324.8 96.8 %reduce-scatter.13.cloned.1.call-done = bf16[256,128]{0,1:T(8,128)(2,1)} async-done(((bf16[2048,128]{0,1:T(8,128)(2,1)}), bf16[256,128]{0,1:T(8,128)(2,1)}) %reduce-scatter.13.cloned.1.call-update) | async-done | bytes 65552 | tf_op jit(solution)/shard_map/reduce_scatter | solution.py:228
  427.2 4.6 while.99
  437.7 49.9 %all-reduce = bf16[3072]{0:T(1024)(128)(2,1)S(1)} all-reduce(bf16[3072]{0:T(1024)(128)(2,1)S(1)} %dynamic-update-slice), channel_id=1, replica_groups=mesh['dp'=4,'seq'=8] {'dp','seq'}, use_global_device_ids=true, to_apply=%add | all-reduce | flops 3072 | bytes 12288
  493.1 11.1 fusion.120
  504.2 48.2 %all-gather.12.cloned.1.call-done = bf16[3072,768]{1,0:T(8,128)(2,1)} async-done(((bf16[96,768]{1,0:T(8,128)(2,1)}), bf16[3072,768]{1,0:T(8,128)(2,1)}) %all-gather.12.cloned.1.call-update) | async-done | bytes 4718608 | tf_op jit(solution)/shard_map/all_gather | solution.py:86
  552.4 7.3 convert_reduce_fusion.1
  563.2 8.1 fusion.123
  575.5 5.2 convolution_add_fusion.1
  583.8 5.2 convolution_add_fusion
  606.1 5.5 fusion.187
  613.3 40.6 %all-reduce.4 = (f32[3072]{0:T(1024)S(1)}, f32[7,768]{1,0:T(8,128)S(1)}, f32[128]{0:T(128)}) all-reduce(f32[3072]{0:T(1024)S(1)} %add.510, f32[7,768]{1,0:T(8,128)S(1)} %add.511, f32[128]{0:T(128)S(1)} %copy-done.70), channel_id=16, replica_groups=mesh['dp'=4,'seq'=8] {'dp','seq'}, use_global_device_ids=true, to_apply=%region_47.48.clone | all-reduce | flops 8576 | bytes 68608
  655.1 4.3 convolution_add_fusion.13
  667.2 89.2 %reduce-scatter.17.cloned.1.call-done = f32[24,768]{1,0:T(8,128)} async-done(((f32[768,768]{1,0:T(8,128)}), f32[24,768]{1,0:T(8,128)}) %reduce-scatter.17.cloned.1.call-update) | async-done | bytes 73744 | tf_op jit(solution)/shard_map/reduce_scatter | solution.py:267
  756.4 103.9 %reduce-scatter.15.cloned.1.call-done = f32[24,768]{1,0:T(8,128)} async-done(((f32[768,768]{1,0:T(8,128)}), f32[24,768]{1,0:T(8,128)}) %reduce-scatter.15.cloned.1.call-update) | async-done | bytes 73744 | tf_op jit(solution)/shard_map/reduce_scatter | solution.py:265
  860.3 142.0 %reduce-scatter.19.cloned.1.call-done = f32[24,3072]{1,0:T(8,128)} async-done(((f32[768,3072]{1,0:T(8,128)}), f32[24,3072]{1,0:T(8,128)}) %reduce-scatter.19.cloned.1.call-update) | async-done | bytes 294928 | tf_op jit(solution)/shard_map/reduce_scatter | solution.py:268
  1002.3 140.9 %reduce-scatter.21.cloned.1.call-done = f32[96,768]{1,0:T(8,128)} async-done(((f32[3072,768]{1,0:T(8,128)}), f32[96,768]{1,0:T(8,128)}) %reduce-scatter.21.cloned.1.call-update) | async-done | bytes 294928 | tf_op jit(solution)/shard_map/reduce_scatter | solution.py:269
  (344 shorter events, 144.5 us)
Async XLA Ops:
  7.2 106.0 %copy-start.2 = (bf16[2,1,256,768]{3,2,1,0:T(8,128)(2,1)S(1)}, bf16[2,1,256,768]{3,2,1,0:T(8,128)(2,1)}, u32[]{:S(2)}) copy-start(bf16[2,1,256,768]{3,2,1,0:T(8,128)(2,1)} %param.27) | copy-start | bytes 2359300
  7.2 105.9 %all-gather.6.cloned.1.call-start = ((), (), s32[]{:S(2)}) async-start(), calls=%async_computation.7 | async-start | bytes 1216512 | tf_op jit(solution)/shard_map/all_gather | solution.py:82
  7.9 116.4 %all-gather.8.cloned.1.call-start = ((), (), s32[]{:S(2)}) async-start(), calls=%async_computation.8 | async-start | bytes 1216512 | tf_op jit(solution)/shard_map/all_gather | solution.py:84
  8.7 253.8 %reduce-scatter.11.cloned.1.call-start = ((), (), s32[]{:S(2)}) async-start(), calls=%async_computation.11 | async-start | bytes 589824 | tf_op jit(solution)/shard_map/reduce_scatter | solution.py:228
  8.7 107.1 %copy-start.67 = (f32[8]{0:T(128)}, f32[8]{0:T(128)S(1)}, u32[]{:S(2)}) copy-start(f32[8]{0:T(128)S(1)} %multiply_power_fusion) | copy-start | bytes 100
  10.0 105.8 %copy-start.66 = (f32[1,1,256]{2,1,0:T(1,128)}, f32[1,1,256]{2,1,0:T(1,128)S(1)}, u32[]{:S(2)}) copy-start(f32[1,1,256]{2,1,0:T(1,128)S(1)} %get-tuple-element.911) | copy-start | bytes 3076
  12.0 103.8 %copy-start.44 = (f32[256]{0:T(256)}, f32[256]{0:T(256)S(1)}, u32[]{:S(2)}) copy-start(f32[256]{0:T(256)S(1)} %get-tuple-element.935) | copy-start | bytes 3076
  12.0 411.4 %copy-start.40 = (f32[256]{0:T(256)}, f32[256]{0:T(256)S(1)}, u32[]{:S(2)}) copy-start(f32[256]{0:T(256)S(1)} %get-tuple-element.934) | copy-start | bytes 3076
  13.5 103.7 %copy-start.53 = (f32[256]{0:T(256)}, f32[256]{0:T(256)S(1)}, u32[]{:S(2)}) copy-start(f32[256]{0:T(256)S(1)} %add_rsqrt_fusion.1) | copy-start | bytes 3076
  95.9 61.1 %copy-start.16 = (bf16[768,128]{1,0:T(8,128)(2,1)}, bf16[768,128]{1,0:T(8,128)(2,1)S(1)}, u32[]{:S(2)}) copy-start(bf16[768,128]{1,0:T(8,128)(2,1)S(1)} %all_gather.19) | copy-start | bytes 589828
  98.1 19.3 %copy-start.30 = (f32[256,8]{0,1:T(8,128)}, f32[256,8]{0,1:T(8,128)S(1)}, u32[]{:S(2)}) copy-start(f32[256,8]{0,1:T(8,128)S(1)} %get-tuple-element.915) | copy-start | bytes 24580
  117.4 6.9 copy-start.3
  156.9 264.7 %reduce-scatter.13.cloned.1.call-start = ((), (), s32[]{:S(2)}) async-start(), calls=%async_computation.12 | async-start | bytes 589824 | tf_op jit(solution)/shard_map/reduce_scatter | solution.py:228
  264.2 58.8 %copy-start.34 = (bf16[256,8]{0,1:T(8,128)(2,1)}, bf16[256,8]{0,1:T(8,128)(2,1)S(1)}, u32[]{:S(2)}) copy-start(bf16[256,8]{0,1:T(8,128)(2,1)S(1)} %get-tuple-element.901) | copy-start | bytes 12292
  264.2 58.8 %copy-start.36 = (bf16[256,8]{0,1:T(8,128)(2,1)}, bf16[256,8]{0,1:T(8,128)(2,1)S(1)}, u32[]{:S(2)}) copy-start(bf16[256,8]{0,1:T(8,128)(2,1)S(1)} %get-tuple-element.902) | copy-start | bytes 12292
  311.6 181.4 %all-gather.10.cloned.1.call-start = ((), (), s32[]{:S(2)}) async-start(), calls=%async_computation.9 | async-start | bytes 4866048 | tf_op jit(solution)/shard_map/all_gather | solution.py:85
  312.2 240.2 %all-gather.12.cloned.1.call-start = ((), (), s32[]{:S(2)}) async-start(), calls=%async_computation.10 | async-start | bytes 4866048 | tf_op jit(solution)/shard_map/all_gather | solution.py:86
  312.8 354.4 %reduce-scatter.23.cloned.1.call-start = ((), (), s32[]{:S(2)}) async-start(), calls=%async_computation.17 | async-start | bytes 405504
  318.1 105.2 %copy-start.65 = (f32[1,1,256]{2,1,0:T(1,128)S(1)}, f32[1,1,256]{2,1,0:T(1,128)}, u32[]{:S(2)}) copy-start(f32[1,1,256]{2,1,0:T(1,128)} %get-tuple-element.912) | copy-start | bytes 3076
  318.1 105.2 %copy-start.68 = (f32[8]{0:T(128)S(1)}, f32[8]{0:T(128)}, u32[]{:S(2)}) copy-start(f32[8]{0:T(128)} %copy-done.67) | copy-start | bytes 100
  318.1 105.8 %copy-start.50 = (f32[256]{0:T(256)S(1)}, f32[256]{0:T(256)}, u32[]{:S(2)}) copy-start(f32[256]{0:T(256)} %copy-done.49) | copy-start | bytes 3076
  426.2 330.2 %reduce-scatter.17.cloned.1.call-start = ((), (), s32[]{:S(2)}) async-start(), calls=%async_computation.14 | async-start | bytes 2433024 | tf_op jit(solution)/shard_map/reduce_scatter | solution.py:267
  437.4 50.9 %copy-start.31 = (f32[256,8]{0,1:T(8,128)S(1)}, f32[256,8]{0,1:T(8,128)}, u32[]{:S(2)}) copy-start(f32[256,8]{0,1:T(8,128)} %copy-done.30) | copy-start | bytes 24580
  437.4 422.9 %reduce-scatter.15.cloned.1.call-start = ((), (), s32[]{:S(2)}) async-start(), calls=%async_computation.13 | async-start | bytes 2433024 | tf_op jit(solution)/shard_map/reduce_scatter | solution.py:265
  492.9 509.4 %reduce-scatter.19.cloned.1.call-start = ((), (), s32[]{:S(2)}) async-start(), calls=%async_computation.15 | async-start | bytes 9732096 | tf_op jit(solution)/shard_map/reduce_scatter | solution.py:268
  493.0 59.3 %copy-start.4 = (bf16[2,1,256,768]{3,2,1,0:T(8,128)(2,1)S(1)}, bf16[2,1,256,768]{3,2,1,0:T(8,128)(2,1)}, u32[]{:S(2)}) copy-start(bf16[2,1,256,768]{3,2,1,0:T(8,128)(2,1)} %param.37) | copy-start | bytes 2359300
  552.4 8.5 copy-start.47
  552.4 8.5 copy-start.56
  560.9 10.5 slice-start
  563.2 8.1 slice-start.1
  580.7 562.5 %reduce-scatter.21.cloned.1.call-start = ((), (), s32[]{:S(2)}) async-start(), calls=%async_computation.16 | async-start | bytes 9732096 | tf_op jit(solution)/shard_map/reduce_scatter | solution.py:269
  611.5 43.6 %copy-start.69 = (f32[768]{0:T(1024)S(1)}, f32[768]{0:T(1024)}, u32[]{:S(2)}) copy-start(f32[768]{0:T(1024)} %get-tuple-element.731) | copy-start | bytes 9220
  (54 other events, 153.1 us)
Sparse Core Ops, SparseCore 0:
  11.0 56.9 all-gather.5
  71.1 53.1 all-gather.7
  157.0 105.3 reduce-scatter.10
  311.7 109.8 reduce-scatter.12
  424.5 62.4 all-gather.9
  489.8 62.4 all-gather.11
  557.9 93.6 reduce-scatter.22
  658.3 98.0 reduce-scatter.16
  762.3 97.9 reduce-scatter.14
  867.6 134.6 reduce-scatter.18
  1008.8 134.4 reduce-scatter.20
where the time goes:
time: 1160 us; the launch traced here: 1150 us
  waiting for transfers between devices  724 us (62%)
  blocking collectives  202 us (17%)
  matrix products  149 us (13%)
  other arithmetic  32.9 us (3%)
  local copies, waits for them, and re-layouts  25.1 us (2%)
  between operations  15.4 us (1%)
    reduce_scatter x2, waiting for transfers between devices, on_device(): lax.psum_scatter(d_shared_all.astype(jnp.bfloat16), 'seq', scatter_dimens...  193 us
    reduce_scatter x1, waiting for transfers between devices, on_device(): lax.psum_scatter(grad_w_up, ('dp', 'seq'), scatter_dimension=0, tiled=True)  142 us
    reduce_scatter x1, waiting for transfers between devices, on_device(): lax.psum_scatter(grad_w_down, ('dp', 'seq'), scatter_dimension=0, tiled=T...  141 us
    reduce_scatter x1, waiting for transfers between devices, on_device(): lax.psum_scatter(grad_w_query, ('dp', 'seq'), scatter_dimension=0, tiled=...  104 us
    unnamed x2, blocking collectives  90.4 us
    reduce_scatter x1, waiting for transfers between devices, on_device(): lax.psum_scatter(grad_w_out, ('dp', 'seq'), scatter_dimension=0, tiled=True)  89.2 us
    all_gather x1, waiting for transfers between devices, on_device(): lax.all_gather(w_down, ('dp', 'seq'), axis=0, tiled=True)  48.2 us
    all_gather x1, blocking collectives, on_device(): lax.all_gather(vectors, ('dp', 'seq'), axis=1, tiled=True)  43.7 us
  transfers between devices with their start and end apart: 11, of which 8 were waited for; matrix products, arithmetic and copies ran while one was open for 12% of the time, Pallas kernels for 0%

commit v1 on v0

--- a/solution.py
+++ b/solution.py
@@ -1,8 +1,11 @@
+import functools
 import math
 
 import jax
 import jax.numpy as jnp
 from jax import lax
+from jax.experimental import pallas as pl
+from jax.experimental.pallas import tpu as pltpu
 from jax.sharding import PartitionSpec as P
 
 H = 12
@@ -54,7 +57,7 @@
     return tuple((left_item + right_item for left_item, right_item in zip(left_tree, right_tree)))
 
 
-def on_device(inputs, offsets, w_query, w_kv, w_out, w_up, w_down, b_up, vectors, b_kv, cotangent):
+def plain_on_device(inputs, offsets, w_query, w_kv, w_out, w_up, w_down, b_up, vectors, b_kv, cotangent):
     micro_count = inputs.shape[0]
     local_rows = inputs.shape[2]
     model_width = inputs.shape[3]
@@ -286,7 +289,504 @@
     )
 
 
+MESH = pl.DeviceIdType.MESH
+NT = (((1,), (1,)), ((), ()))
+VM = pl.BlockSpec(memory_space=pltpu.VMEM)
+HBM = pl.BlockSpec(memory_space=pl.ANY)
+GROUP = 4
+KEYS = 512
+MINI = 256
+scale_log2 = 0.125 * 1.4426950408889634
+
+
+def dot(left, right):
+    return jnp.dot(left, right, preferred_element_type=jnp.float32)
+
+
+def dot_nt(left, right):
+    return lax.dot_general(left, right, NT, preferred_element_type=jnp.float32)
+
+
+def bf(values):
+    return values.astype(jnp.bfloat16)
+
+
+def f32(values):
+    return values.astype(jnp.float32)
+
+
+def rotate_rows(block, cosine, sine_part):
+    half_rot = ROT // 2
+    first, second = block[:half_rot], block[half_rot:ROT]
+    return jnp.concatenate(
+        [first * cosine - second * sine_part, second * cosine + first * sine_part, block[ROT:]],
+        axis=0,
+    )
+
+
+def here():
+    return lax.axis_index("dp"), lax.axis_index("seq")
+
+
+def greet(targets):
+    barrier = pltpu.get_barrier_semaphore()
+    for target in targets:
+        pl.semaphore_signal(barrier, inc=1, device_id=target, device_id_type=MESH)
+    pl.semaphore_wait(barrier, len(targets))
+
+
+def remote(source, target, send, recv, device):
+    return pltpu.make_async_remote_copy(
+        src_ref=source,
+        dst_ref=target,
+        send_sem=send,
+        recv_sem=recv,
+        device_id=device,
+        device_id_type=MESH,
+    )
+
+
+class Gather:
+    def __init__(self, shard, slabs, halves, send, recv):
+        self.shard, self.slabs, self.halves, self.send, self.recv = shard, slabs, halves, send, recv
+        self.dp, self.seq = here()
+        self.sent = []
+
+    def index(self, dp_flip, z_flip, core_flip=0):
+        return (self.dp ^ dp_flip) * 8 + (self.seq ^ (2 * z_flip + core_flip))
+
+    def part(self, slab, half):
+        rows, columns = half
+        return self.slabs.at[slab, rows, columns]
+
+    def start(self, number, source, target, device):
+        copy = remote(source, target, self.send.at[number], self.recv.at[number], device)
+        copy.start()
+        self.sent.append(copy)
+
+    def arrived(self, number, target):
+        remote(target, target, self.send.at[number], self.recv.at[number], (self.dp, self.seq ^ 1)).wait_recv()
+
+    def own(self):
+        mine = self.slabs.at[self.index(0, 0)]
+        for flip in (1, 2, 3):
+            self.start(flip - 1, self.shard, mine, (self.dp, self.seq ^ (2 * flip)))
+        self.start(3, self.shard, mine, (self.dp ^ 1, self.seq))
+        self.start(7, self.shard, mine, (self.dp ^ 2, self.seq))
+        self.start(19, self.shard, mine, (self.dp, self.seq ^ 1))
+
+    def from_z(self, flip):
+        piece = self.slabs.at[self.index(0, flip)]
+        self.arrived(flip - 1, piece)
+        self.start(3 + flip, piece, piece, (self.dp ^ 1, self.seq))
+        self.start(7 + flip, piece, piece, (self.dp ^ 2, self.seq))
+        self.start(19 + flip, piece, piece, (self.dp, self.seq ^ 1))
+
+    def from_xy(self, flip):
+        for axis, half in ((1, 0), (2, 1)):
+            number = 3 if axis == 1 else 7
+            slab = self.index(axis, flip)
+            piece = self.slabs.at[slab]
+            self.arrived(number + flip, piece)
+            cut = self.part(slab, self.halves[half])
+            self.start(11 + 4 * half + flip, cut, cut, (self.dp ^ (3 - axis), self.seq))
+            self.start((23 if axis == 1 else 27) + flip, piece, piece, (self.dp, self.seq ^ 1))
+
+    def from_diagonal(self, flip):
+        slab = self.index(3, flip)
+        for half in (0, 1):
+            self.arrived(11 + 4 * half + flip, self.part(slab, self.halves[half]))
+        piece = self.slabs.at[slab]
+        self.start(31 + flip, piece, piece, (self.dp, self.seq ^ 1))
+
+    def from_core(self):
+        for number, dp_flip in ((19, 0), (23, 1), (27, 2), (31, 3)):
+            for flip in range(4):
+                self.arrived(number + flip, self.slabs.at[self.index(dp_flip, flip, 1)])
+
+    def finish(self):
+        for copy in self.sent:
+            copy.wait_send()
+
+
+def attend(
+    micro, steps, row0, begin_ref, q_t, do_t, kv_ref, kv_t, att_t, dq_t, dkv, pair, scaled, score_ref, weight_ref, tick
+):
+    cols = slice(micro * MINI, (micro + 1) * MINI)
+    begin = begin_ref[0:1, cols]
+    row_ids = row0 + lax.broadcasted_iota(jnp.int32, (1, MINI), 1)
+    for group in range(H // GROUP):
+        heads = [slice((group * GROUP + n) * HD, (group * GROUP + n + 1) * HD) for n in range(GROUP)]
+        for n, head in enumerate(heads):
+            pair[n, :HD, :MINI] = q_t[head, cols]
+            pair[n, HD:, MINI:] = do_t[head, cols]
+
+        def score_step(step, tops):
+            keys = pl.ds(pl.multiple_of(step * KEYS, KEYS), KEYS)
+            block = kv_ref[micro, keys, :]
+            ids = step * KEYS + lax.broadcasted_iota(jnp.int32, (KEYS, 1), 0)
+            allowed = (ids <= row_ids) & (ids >= begin)
+            found = []
+            for n in range(GROUP):
+                both = dot(block, pair[n])
+                scores = jnp.where(allowed, both[:, :MINI] * scale_log2, masked_score)
+                score_ref[n, keys, :MINI] = scores
+                score_ref[n, keys, MINI:] = both[:, MINI:]
+                found.append(jnp.maximum(tops[n], jnp.max(scores.reshape(KEYS // 8, 8, MINI), axis=0)))
+            return tuple(found)
+
+        tops = lax.fori_loop(
+            0, steps, score_step, tuple(jnp.full((8, MINI), masked_score, jnp.float32) for _ in heads)
+        )
+        tops = [jnp.max(top, axis=0, keepdims=True) for top in tops]
+
+        def value_step(step, carried):
+            keys = pl.ds(pl.multiple_of(step * KEYS, KEYS), KEYS)
+            values = kv_t[micro, HD:, keys]
+            found = []
+            for n in range(GROUP):
+                output, total = carried[n]
+                weights = jnp.exp2(score_ref[n, keys, :MINI] - tops[n])
+                total = total + jnp.sum(weights.reshape(KEYS // 8, 8, MINI), axis=0)
+                weight_ref[n, keys, :] = bf(weights)
+                found.append((output + dot(values, bf(weights)), total))
+            return tuple(found)
+
+        sums = lax.fori_loop(
+            0,
+            steps,
+            value_step,
+            tuple((jnp.zeros((HD, MINI), jnp.float32), jnp.zeros((8, MINI), jnp.float32)) for _ in heads),
+        )
+        inverses, deltas = [], []
+        for n, head in enumerate(heads):
+            inverse = 1.0 / jnp.sum(sums[n][1], axis=0, keepdims=True)
+            output = sums[n][0] * inverse
+            upstream = f32(do_t[head, cols])
+            deltas.append(jnp.sum(output * upstream, axis=0, keepdims=True))
+            inverses.append(inverse)
+            att_t[head, cols] = bf(output)
+            scaled[n, :HD, :MINI] = bf(f32(q_t[head, cols]) * inverse)
+            scaled[n, HD:, MINI:] = bf(upstream * inverse)
+
+        def grad_step(step, carried):
+            keys = pl.ds(pl.multiple_of(step * KEYS, KEYS), KEYS)
+            key_block = kv_t[micro, :HD, keys]
+            total = dkv[micro, keys, :]
+            found = []
+            for n in range(GROUP):
+                weights = weight_ref[n, keys, :]
+                d_scores = bf(f32(weights) * (score_ref[n, keys, MINI:] - deltas[n]))
+                found.append(carried[n] + dot(key_block, d_scores))
+                total = total + dot_nt(d_scores, scaled[n, :, :MINI])
+                total = total + dot_nt(weights, scaled[n, :, MINI:])
+            dkv[micro, keys, :] = total
+            return tuple(found)
+
+        grads = lax.fori_loop(
+            0, steps, grad_step, tuple(jnp.zeros((HD, MINI), jnp.float32) for _ in heads)
+        )
+        for n, head in enumerate(heads):
+            dq_t[head, cols] = grads[n] * (inverses[n] * 0.125)
+        tick(micro, group)
+
+
+def spread(slabs):
+    lane = lax.broadcasted_iota(jnp.int32, (8, 128), 1)
+    row = lax.broadcasted_iota(jnp.int32, (8, 128), 0)
+    rows = [jnp.zeros((8, 128), jnp.float32) for _ in range(6)]
+    wide = [jnp.zeros((8, 128), jnp.float32) for _ in range(24)]
+    for number in range(32):
+        for width, target, keep in ((24, rows, row < 7), (96, wide, row == 7)):
+            block, shift = divmod(number * width, 128)
+            piece = jnp.where(keep, slabs[number], 0.0)
+            piece = pltpu.roll(piece, shift, 1) if shift else piece
+            target[block] = target[block] + jnp.where(lane >= shift, piece, 0.0)
+            if shift + width > 128:
+                target[block + 1] = target[block + 1] + jnp.where(lane < shift, piece, 0.0)
+    return jnp.concatenate(rows, axis=1), jnp.concatenate(wide, axis=1)
+
+
+def slab_order(store, block, dp_index, rows):
+    for z in range(4):
+        for core in range(2):
+            first = (2 * z + core) * rows
+            store(dp_index, core, z, bf(block[first : first + rows]))
+
+
+def attention_kernel(
+    x_ref, cot_ref, begin_ref, cos_ref, sin_ref, bkv_ref, small_ref, up_ref, down_ref,
+    up_slabs, down_slabs, vec_ref, bup_ref, wkv_ref, attn_ref, dn_ref, dkv_out, grads_ref, dqsum_ref,
+    slabs, weights, n1_ref, n1t_ref, q_t, do_t, att_t, dq_t, kv_ref, kv_t, dkv, pair, scaled, score_ref, weight_ref,
+    send_a, recv_a, send_u, recv_u, send_d, recv_d, send_kv, recv_kv, local_sem,
+):
+    dp, seq = here()
+    wide = slabs.shape[2] // 2
+    gather_a = Gather(small_ref, slabs, ((slice(None), slice(0, wide)), (slice(None), slice(wide, 2 * wide))), send_a, recv_a)
+    half = up_ref.shape[1] // 2
+    gather_u = Gather(up_ref, up_slabs, ((slice(None), slice(0, half)), (slice(None), slice(half, 2 * half))), send_u, recv_u)
+    half = down_ref.shape[0] // 2
+    gather_d = Gather(down_ref, down_slabs, ((slice(0, half), slice(None)), (slice(half, 2 * half), slice(None))), send_d, recv_d)
+    greet(
+        [(dp, seq ^ 1), (dp, seq ^ 2), (dp, seq ^ 4), (dp, seq ^ 6), (dp ^ 1, seq), (dp ^ 2, seq)]
+    )
+    gather_a.own()
+    mine = gather_a.index(0, 0)
+    local_copies = [
+        pltpu.make_async_copy(small_ref, slabs.at[mine], local_sem.at[0]),
+        pltpu.make_async_copy(up_ref, up_slabs.at[mine], local_sem.at[1]),
+        pltpu.make_async_copy(down_ref, down_slabs.at[mine], local_sem.at[2]),
+    ]
+    for copy in local_copies:
+        copy.start()
+    pair[...] = jnp.zeros_like(pair)
+    scaled[...] = jnp.zeros_like(scaled)
+    dkv[...] = jnp.zeros_like(dkv)
+    normed, _ = normalize(f32(x_ref[...]))
+    for flip in (1, 2, 3):
+        gather_a.from_z(flip)
+    for flip in range(4):
+        gather_a.from_xy(flip)
+    for flip in range(4):
+        gather_a.from_diagonal(flip)
+    gather_a.from_core()
+    local_copies[0].wait()
+
+    for number in range(16):
+        block = jnp.concatenate([f32(slabs[2 * number]), f32(slabs[2 * number + 1])], axis=0)
+        weights[48 * number : 48 * number + 48, :] = bf(block)
+    vectors, wide_row = spread([f32(slabs[number, 0:8, 896:1024]) for number in range(32)])
+    vec_ref[...] = vectors
+    bup_ref[...] = wide_row[7:8]
+    wkv_ref[...] = weights[:, 768:896]
+
+    hidden = bf(normed * vectors[0:1] + vectors[1:2])
+    n1_ref[...] = hidden
+    kv_pre = dot(hidden, weights[:, 768:896]) + bkv_ref[...]
+    kv_pre_t = kv_pre.T
+    cosine, sine_part = cos_ref[...], sin_ref[...]
+    shared_t = bf(jnp.concatenate([rotate_rows(kv_pre_t[:HD], cosine, sine_part), kv_pre_t[HD:]], axis=0))
+    shared = bf(f32(shared_t).T)
+    place = pl.ds(pl.multiple_of(seq * MINI, MINI), MINI)
+    kv_copies = []
+    for micro in range(2):
+        kv_ref[micro, place, :] = shared[micro * MINI : (micro + 1) * MINI]
+
+    def kv_block(micro, flip):
+        return kv_ref.at[micro, pl.ds(pl.multiple_of((seq ^ flip) * MINI, MINI), MINI)]
+
+    def kv_send(micro, flip, number, device):
+        block = kv_block(micro, flip)
+        copy = remote(block, block, send_kv.at[micro, number], recv_kv.at[micro, number], device)
+        copy.start()
+        kv_copies.append(copy)
+
+    def kv_arrived(micro, flip, number):
+        block = kv_block(micro, flip)
+        remote(block, block, send_kv.at[micro, number], recv_kv.at[micro, number], (dp, seq ^ 1)).wait_recv()
+
+    for micro in range(2):
+        for flip in (1, 2, 3):
+            kv_send(micro, 0, flip - 1, (dp, seq ^ (2 * flip)))
+        kv_send(micro, 0, 3, (dp, seq ^ 1))
+    gather_u.own()
+    gather_d.own()
+
+    n1t_ref[...] = bf(f32(hidden).T)
+    query = (dot(hidden, weights[:, :768]) + vectors[4:5]).T
+    for head in range(H):
+        q_t[head * HD : (head + 1) * HD, :] = bf(
+            rotate_rows(query[head * HD : (head + 1) * HD], cosine, sine_part)
+        )
+    do_t[...] = bf(dot_nt(weights[:, 1024:1792], cot_ref[...]))
+
+    def kv_forward(micro):
+        for flip in (1, 2, 3):
+            kv_arrived(micro, 2 * flip, flip - 1)
+            kv_send(micro, 2 * flip, 3 + flip, (dp, seq ^ 1))
+
+    def kv_finish(micro):
+        for flip in range(4):
+            kv_arrived(micro, 2 * flip + 1, 3 + flip)
+        kv_t[micro] = bf(f32(kv_ref[micro]).T)
+
+    kv_forward(0)
+    kv_forward(1)
+    kv_finish(0)
+
+    def tick(micro, group):
+        at = micro * (H // GROUP) + group
+        if at == 0:
+            gather_u.from_z(1)
+            gather_d.from_z(1)
+        if at == 1:
+            gather_u.from_z(2)
+            gather_d.from_z(2)
+            gather_u.from_z(3)
+            gather_d.from_z(3)
+        if at == 2:
+            for flip in (0, 1):
+                gather_u.from_xy(flip)
+                gather_d.from_xy(flip)
+        if at == 3:
+            for flip in (2, 3):
+                gather_u.from_xy(flip)
+                gather_d.from_xy(flip)
+        if at == 4:
+            for flip in range(4):
+                gather_u.from_diagonal(flip)
+                gather_d.from_diagonal(flip)
+
+    steps = lax.div((seq + 1) * MINI + KEYS - 1, KEYS)
+    for micro in range(2):
+        if micro == 1:
+            kv_finish(1)
+        attend(
+            micro, steps, seq * MINI, begin_ref, q_t, do_t, kv_ref, kv_t, att_t, dq_t, dkv,
+            pair, scaled, score_ref, weight_ref, tick,
+        )
+    for micro in range(2):
+        for core in range(2):
+            for z in range(4):
+                first = (2 * z + core) * MINI
+                block = dkv[micro, first : first + MINI, :]
+                scale = jnp.where(lax.broadcasted_iota(jnp.int32, (1, 2 * HD), 1) < HD, 0.125, 1.0)
+                dkv_out[core, z, micro] = bf(block * scale)
+    attn_ref[...] = dot(bf(f32(att_t[...]).T), weights[:, 1024:1792]) + vectors[5:6]
+    for head in range(H):
+        dq_t[head * HD : (head + 1) * HD, :] = rotate_rows(
+            dq_t[head * HD : (head + 1) * HD, :], cosine, -sine_part
+        )
+    d_query = bf(dq_t[...].T)
+    dqsum_ref[...] = jnp.sum(f32(d_query), axis=0, keepdims=True)
+    dn_ref[...] = dot_nt(d_query, weights[:, :768])
+    for block in range(4):
+        rows = slice(192 * block, 192 * block + 192)
+
+        def put_query(dp_index, core, z, piece):
+            grads_ref[dp_index, core, z, :, 0:768] = piece
+
+        def put_out(dp_index, core, z, piece):
+            grads_ref[dp_index, core, z, :, 768:1536] = piece
+
+        slab_order(put_query, dot(n1t_ref[rows, :], d_query), block, 24)
+        slab_order(put_out, dot(att_t[rows, :], cot_ref[...]), block, 24)
+    for gather in (gather_u, gather_d):
+        gather.from_core()
+    for gather in (gather_a, gather_u, gather_d):
+        gather.finish()
+    for copy in kv_copies:
+        copy.wait_send()
+    for copy in local_copies[1:]:
+        copy.wait()
+
+
+def attention_call(x, cot, begin, cosine, sine_part, b_kv, small, w_up, w_down):
+    rows = x.shape[0]
+    dma = pltpu.SemaphoreType.DMA
+    out = lambda shape, kind: jax.ShapeDtypeStruct(shape, kind)
+    seqlen = 8 * MINI
+    return pl.pallas_call(
+        attention_kernel,
+        out_shape=(
+            out((32,) + w_up.shape, jnp.bfloat16),
+            out((32,) + w_down.shape, jnp.bfloat16),
+            out((8, 768), jnp.float32),
+            out((1, 3072), jnp.float32),
+            out((768, 128), jnp.bfloat16),
+            out((rows, 768), jnp.float32),
+            out((rows, 768), jnp.float32),
+            out((2, 4, 2, MINI, 2 * HD), jnp.bfloat16),
+            out((4, 2, 4, 24, 1536), jnp.bfloat16),
+            out((1, 768), jnp.float32),
+        ),
+        in_specs=[VM] * 7 + [HBM] * 2,
+        out_specs=(HBM, HBM) + (VM,) * 8,
+        scratch_shapes=[
+            pltpu.VMEM((32,) + small.shape, jnp.bfloat16),
+            pltpu.VMEM((768, small.shape[1]), jnp.bfloat16),
+            pltpu.VMEM((rows, 768), jnp.bfloat16),
+            pltpu.VMEM((768, rows), jnp.bfloat16),
+            pltpu.VMEM((768, rows), jnp.bfloat16),
+            pltpu.VMEM((768, rows), jnp.bfloat16),
+            pltpu.VMEM((768, rows), jnp.bfloat16),
+            pltpu.VMEM((768, rows), jnp.float32),
+            pltpu.VMEM((2, seqlen, 2 * HD), jnp.bfloat16),
+            pltpu.VMEM((2, 2 * HD, seqlen), jnp.bfloat16),
+            pltpu.VMEM((2, seqlen, 2 * HD), jnp.float32),
+            pltpu.VMEM((GROUP, 2 * HD, 2 * MINI), jnp.bfloat16),
+            pltpu.VMEM((GROUP, 2 * HD, 2 * MINI), jnp.bfloat16),
+            pltpu.VMEM((GROUP, seqlen, 2 * MINI), jnp.float32),
+            pltpu.VMEM((GROUP, seqlen, MINI), jnp.bfloat16),
+        ]
+        + [dma((35,))] * 6
+        + [dma((2, 7))] * 2
+        + [dma((3,))],
+        compiler_params=pltpu.CompilerParams(
+            collective_id=0, has_side_effects=True, vmem_limit_bytes=60 << 20
+        ),
+        name="attention",
+    )(x, cot, begin, cosine, sine_part, b_kv, small, w_up, w_down)
+
+
+def packed_on_device(inputs, offsets, w_query, w_kv, w_out, w_up, w_down, b_up, vectors, b_kv, cotangent):
+    rows = 2 * MINI
+    seq = lax.axis_index("seq")
+    x = inputs.reshape(rows, 768)
+    cot = cotangent.reshape(rows, 768)
+    flat_offsets = offsets.reshape(1, rows)
+    places = seq * MINI + lax.rem(lax.broadcasted_iota(jnp.int32, (1, rows), 1), MINI)
+    begin = places - flat_offsets
+    frequency = jnp.power(10000.0, -jnp.arange(ROT // 2, dtype=jnp.float32) * (2.0 / ROT))
+    angle = (flat_offsets.astype(jnp.float32) * 0.25) * frequency[:, None]
+    cosine, sine_part = jnp.cos(angle), jnp.sin(angle)
+    per_row = vectors.shape[1]
+    extra = jnp.zeros((24, 128), jnp.bfloat16)
+    extra = extra.at[:7, :per_row].set(vectors).at[7, : b_up.shape[0]].set(b_up)
+    small = jnp.concatenate([w_query, w_kv, extra, w_out], axis=1)
+    up_slabs, down_slabs, vec, bup, wkv, attn, dn1, dkv, grads_a, dq_sum = attention_call(
+        x, cot, begin, cosine, sine_part, b_kv.reshape(1, -1).astype(jnp.float32), small, w_up, w_down
+    )
+    return feed_forward(x, cot, cosine, sine_part, up_slabs, down_slabs, vec, bup, wkv, attn, dn1, dkv, grads_a, dq_sum)
+
+
+def feed_forward(x, cot, cosine, sine_part, up_slabs, down_slabs, vec, bup, wkv, attn, dn1, dkv, grads_a, dq_sum):
+    up = up_slabs.reshape(768, 3072)
+    down = down_slabs.reshape(3072, 768)
+    xf, cf = f32(x), f32(cot)
+    normed, inverse = normalize(xf)
+    h1 = bf(normed * vec[0] + vec[1])
+    h2 = bf(normed * vec[2] + vec[3])
+    hidden = dot(h2, up) + bup
+    act = bf(jax.nn.gelu(hidden, approximate=False))
+    out = bf(xf + attn + dot(act, down) + vec[6])
+    g_down = dot(act.T, cot)
+    d_hidden = bf(dot_nt(cot, down) * gelu_slope(hidden))
+    g_up = dot(h2.T, d_hidden)
+    g_bup = jnp.sum(f32(d_hidden), axis=0)
+    dn2 = dot_nt(d_hidden, up)
+    pieces = jnp.transpose(dkv, (1, 0, 2, 3, 4)).reshape(8, 2, MINI, 2 * HD)
+    dsh = f32(lax.psum_scatter(pieces, "seq", scatter_dimension=0, tiled=True)).reshape(2 * MINI, 2 * HD)
+    d_shared = bf(jnp.concatenate([rotate(dsh[:, :HD], cosine.T, -sine_part.T), dsh[:, HD:]], axis=1))
+    g_kv = dot(h1.T, d_shared)
+    dn1 = dn1 + dot_nt(d_shared, wkv)
+    g_bkv = lax.psum(jnp.sum(f32(d_shared), axis=0), ("dp", "seq"))
+    csum = jnp.sum(cf, axis=0)
+    g_vec = jnp.stack([jnp.sum(dn1 * normed, axis=0), jnp.sum(dn1, axis=0), jnp.sum(dn2 * normed, axis=0), jnp.sum(dn2, axis=0), dq_sum[0], csum, csum])
+    g_in = cf + norm_back(dn1, normed, inverse, vec[0]) + norm_back(dn2, normed, inverse, vec[2])
+    ga = jnp.transpose(grads_a, (0, 2, 1, 3, 4)).reshape(768, 1536)
+    sc = lambda v, d=0: f32(lax.psum_scatter(v, ("dp", "seq"), scatter_dimension=d, tiled=True))
+    gaq = sc(ga)
+    return (
+        out.reshape(2, 1, MINI, 768), g_in.reshape(2, 1, MINI, 768), gaq[:, :768], sc(bf(g_kv)), gaq[:, 768:],
+        sc(bf(g_up)), sc(bf(g_down)), sc(g_bup), sc(g_vec, 1), g_bkv,
+    )
+
+
 def solution(mesh):
+    packed = mesh.shape["dp"] == 4 and mesh.shape["seq"] == 8
+    on_device = packed_on_device if packed else plain_on_device
+
     in_specs = (
         P(None, "dp", "seq", None),
         P(None, "dp", "seq"),

time: 1160 us -> 582 us (0.50)
  waiting for transfers between devices: 724 us -> 348 us
  blocking collectives: 202 us -> 38.6 us
  matrix products: 149 us -> 51.4 us
  Pallas kernels: 0 us -> 94.7 us
  other arithmetic: 32.9 us -> 14.4 us
  local copies, waits for them, and re-layouts: 25.1 us -> 11.2 us
    reduce_scatter x6 -> x4, waiting for transfers between devices: 669 us -> 348 us  [the longest x3 309 us: feed_forward(): lax.psum_scatter(v, ('dp', 'seq'), scatter_dimension=d, tiled=True)]
    all_gather x4 -> x0, blocking collectives: 111 us -> none  [the longest x1 43.7 us: on_device(): lax.all_gather(vectors, ('dp', 'seq'), axis=1, tiled=True)]
    dot_general x48 -> x8, matrix products: 149 us -> 51.4 us  [the longest x5 36.7 us: dot(): return jnp.dot(left, right, preferred_element_type=jnp.float32)]
    pallas_call x0 -> x1, Pallas kernels: none -> 94.7 us  [attention_call(): pl.pallas_call(attention_kernel, out_shape=(out((32,) + w_up.shape, jnp.b...]
    all_gather x4 -> x0, waiting for transfers between devices: 52.4 us -> none  [the longest x1 48.2 us: on_device(): lax.all_gather(w_down, ('dp', 'seq'), axis=0, tiled=True)]
    unnamed x2 -> x1, blocking collectives: 90.4 us -> 38.6 us
  transfers between devices with their start and end apart: 11 -> 5, of which waited for: 8 -> 4; matrix products, arithmetic and copies ran while one was open for 12% -> 11% of each run, Pallas kernels for 0% -> 0%
where the time goes in v1:
time: 582 us; the launch traced here: 573 us
  waiting for transfers between devices  348 us (60%)
  Pallas kernels  94.7 us (16%)
  matrix products  51.4 us (9%)
  blocking collectives  38.6 us (7%)
  between operations  14.5 us (2%)
  other arithmetic  14.4 us (2%)
  local copies, waits for them, and re-layouts  11.2 us (2%)
    reduce_scatter x3, waiting for transfers between devices, feed_forward(): lax.psum_scatter(v, ('dp', 'seq'), scatter_dimension=d, tiled=True)  309 us
    pallas_call x1, Pallas kernels, attention_call(): pl.pallas_call(attention_kernel, out_shape=(out((32,) + w_up.shape, jnp.b...  94.7 us
    reduce_scatter x1, waiting for transfers between devices, feed_forward(): lax.psum_scatter(pieces, 'seq', scatter_dimension=0, tiled=True)  38.7 us
    unnamed x1, blocking collectives  38.6 us
    dot_general x5, matrix products, dot(): return jnp.dot(left, right, preferred_element_type=jnp.float32)  36.7 us
    dot_general x3, matrix products, dot_nt(): return lax.dot_general(left, right, NT, preferred_element_type=jnp.float32)  14.7 us
  transfers between devices with their start and end apart: 5, of which 4 were waited for; matrix products, arithmetic and copies ran while one was open for 11% of the time, Pallas kernels for 0%

profile of v1, /device:TPU:0, one launch (start us, length us, event | category | flops | bytes accessed | tf_op | source)
XLA Modules:
  0.0 573.4 jit_solution(16309908298334576466)
XLA Ops:
  7.3 1.2 bitcast_convert_fusion.bkv_ref
  8.5 0.7 convert_multiply_fusion
  9.2 1.3 add_subtract_fusion.begin_ref
  10.4 0.7 scatter.6
  11.1 0.8 multiply_sine_fusion.1
  11.9 0.8 scatter.9
  12.6 1.4 pad_maximum_fusion.1.small_ref
  14.1 94.7 %attention.1 = (bf16[32,24,3072]{2,1,0:T(8,128)(2,1)}, bf16[32,96,768]{2,1,0:T(8,128)(2,1)}, f32[8,768]{1,0:T(8,128)}, f32[1,3072]{1,0:T(1,128)}, bf16[768,128]{...) custom-call(bf16[512,768]{1,0:T(8,128)(2,1)} %bitcast.51, ...), custom_call_target="tpu_custom_call" | custom-call | tf_op jit(solution)/shard_map/attention/pallas_call | solution.py:689
  108.9 2.4 copy.31
  112.0 38.7 %reduce-scatter.9.cloned.1.call-done = bf16[1,2,256,128]{3,2,1,0:T(8,128)(2,1)} async-done(((bf16[8,2,256,128]{3,2,1,0:T(8,128)(2,1)}), bf16[1,2,256,128]{3,2,1,0:T(8,128)(2,1)}) %reduce-scatter.9.cloned.1.call-update) | async-done | bytes 131088 | tf_op jit(solution)/shard_map/reduce_scatter | solution.py:769
  150.8 1.0 copy.36
  152.0 1.4 convolution_convert_fusion.2
  153.4 1.8 copy.33
  155.8 17.9 %fusion.2 = (bf16[512,3072]{1,0:T(8,128)(2,1)}, f32[512,3072]{1,0:T(8,128)S(1)}) fusion(f32[3072]{0:T(1024)S(1)} %bitcast.81, bf16[512,768]{1,0:T(8,128)(2,1)S(1)} %bitcast.63, bf16[768,3072]{1,0:T(8,128)(2,1)} %bitcast.79), kind=kOutput, calls=%fused_computation.4 | convolution fusion | flops 2519728128 | bytes 14954496 | tf_op jit(solution)/shard_map/dot_general | solution.py:303
  173.8 6.2 %convert_reduce_fusion = (f32[3072]{0:T(1024)S(1)}, bf16[512,3072]{1,0:T(8,128)(2,1)S(1)}) fusion(f32[512,3072]{1,0:T(8,128)S(1)} %get-tuple-element.125, f32[3072]{0:T(1024)S(1)} %bitcast.82, bf16[3072,768]{1,0:T(8,128)(2,1)} %bitcast.77, bf16[512,768]{1,0:T(8,128)(2,1)S(1)} %bitcast.57), kind=kOutput, calls=%fused_computation.10 | convolution fusion | flops 2436363264 | bytes 14966784 | tf_op jit(solution)/shard_map/dot_general | solution.py:307
  180.0 1.6 copy-done.10
  181.7 4.8 convolution_convert_fusion.1
  186.8 6.7 %convolution_convert_fusion = bf16[3072,768]{1,0:T(8,128)(2,1)} fusion(bf16[512,3072]{1,0:T(8,128)(2,1)} %get-tuple-element.124, bf16[512,768]{1,0:T(8,128)(2,1)S(1)} %bitcast.58), kind=kOutput, calls=%fused_computation.26 | convolution fusion | flops 2418278400 | bytes 8650752 | tf_op jit(solution)/shard_map/dot_general | solution.py:303
  193.6 6.1 %fusion.69 = f32[512,768]{1,0:T(8,128)S(1)} fusion(bf16[512,3072]{1,0:T(8,128)(2,1)} %copy-done.10, bf16[768,3072]{1,0:T(8,128)(2,1)} %bitcast.80), kind=kOutput, calls=%fused_computation.112 | convolution fusion | flops 2415919104 | bytes 9437184 | tf_op jit(solution)/shard_map/dot_general | solution.py:307
  199.8 6.0 %fusion.23 = bf16[512,768]{1,0:T(8,128)(2,1)} fusion(f32[512,768]{1,0:T(8,128)S(1)} %copy-done.6, bf16[512,768]{1,0:T(8,128)(2,1)S(1)} %bitcast.54, bf16[512,3072]{1,0:T(8,128)(2,1)S(1)} %copy-done.9, bf16[3072,768]{1,0:T(8,128)(2,1)} %bitcast.78, f32[768]{0:T(1024)S(1)} %get-tuple-element.108), kind=kOutput, calls=%fused_computation.40 | convolution fusion | flops 2417885184 | bytes 11013120 | tf_op jit(solution)/shard_map/dot_general | solution.py:303
  205.8 2.4 fusion.45
  208.3 38.6 %all-reduce.4 = (f32[3072]{0:T(1024)S(1)}, f32[7,768]{1,0:T(8,128)S(1)}, f32[128]{0:T(128)}) all-reduce(f32[3072]{0:T(1024)S(1)} %get-tuple-element.127, f32[7,768]{1,0:T(8,128)S(1)} %stack.24, f32[128]{0:T(128)S(1)} %convert_reduce_fusion.3), channel_id=7, replica_groups=mesh['dp'=4,'seq'=8] {'dp','seq'}, use_global_device_ids=true, to_apply=%region_12.0.clone | all-reduce | flops 8576 | bytes 68608
  247.0 0.6 dynamic-slice.16
  247.5 0.7 constant_dynamic-slice_fusion
  248.2 3.0 fusion.37
  251.3 1.3 convert_element_type.91
  252.6 88.5 %reduce-scatter.11.cloned.1.call-done = bf16[24,1536]{1,0:T(8,128)(2,1)} async-done(((bf16[768,1536]{1,0:T(8,128)(2,1)}), bf16[24,1536]{1,0:T(8,128)(2,1)}) %reduce-scatter.11.cloned.1.call-update) | async-done | bytes 73744 | tf_op jit(solution)/shard_map/reduce_scatter | solution.py:778
  341.0 1.4 fusion.68
  342.5 110.0 %reduce-scatter.13.cloned.1.call-done = bf16[24,3072]{1,0:T(8,128)(2,1)} async-done(((bf16[768,3072]{1,0:T(8,128)(2,1)}), bf16[24,3072]{1,0:T(8,128)(2,1)}) %reduce-scatter.13.cloned.1.call-update) | async-done | bytes 147472 | tf_op jit(solution)/shard_map/reduce_scatter | solution.py:778
  452.4 1.6 convert_element_type.94
  454.1 110.7 %reduce-scatter.15.cloned.1.call-done = bf16[96,768]{1,0:T(8,128)(2,1)} async-done(((bf16[3072,768]{1,0:T(8,128)(2,1)}), bf16[96,768]{1,0:T(8,128)(2,1)}) %reduce-scatter.15.cloned.1.call-update) | async-done | bytes 147472 | tf_op jit(solution)/shard_map/reduce_scatter | solution.py:778
  564.8 1.6 convert_element_type.96
  (54 shorter events, 2.3 us)
Async XLA Ops:
  7.2 104.2 %copy-start = (bf16[2,1,256,768]{3,2,1,0:T(8,128)(2,1)S(1)}, bf16[2,1,256,768]{3,2,1,0:T(8,128)(2,1)}, u32[]{:S(2)}) copy-start(bf16[2,1,256,768]{3,2,1,0:T(8,128)(2,1)} %param.15) | copy-start | bytes 2359300
  7.2 143.6 %reduce-scatter.9.cloned.1.call-start = ((), (), s32[]{:S(2)}) async-start(), calls=%async_computation.5 | async-start | bytes 1179648 | tf_op jit(solution)/shard_map/reduce_scatter | solution.py:769
  108.8 3.1 copy-start.3
  108.8 44.6 %copy-start.2 = (bf16[4,2,4,24,1536]{4,3,2,1,0:T(8,128)(2,1)S(1)}, bf16[4,2,4,24,1536]{4,3,2,1,0:T(8,128)(2,1)}, u32[]{:S(2)}) copy-start(bf16[4,2,4,24,1536]{4,3,2,1,0:T(8,128)(2,1)} %get-tuple-element.52) | copy-start | bytes 7077892
  111.3 139.9 %reduce-scatter.17.cloned.1.call-start = ((), (), s32[]{:S(2)}) async-start(), calls=%async_computation.9 | async-start | bytes 202752
  153.3 2.5 copy-start.8
  153.4 187.7 %reduce-scatter.11.cloned.1.call-start = ((), (), s32[]{:S(2)}) async-start(), calls=%async_computation.6 | async-start | bytes 2433024 | tf_op jit(solution)/shard_map/reduce_scatter | solution.py:778
  155.2 297.3 %reduce-scatter.13.cloned.1.call-start = ((), (), s32[]{:S(2)}) async-start(), calls=%async_computation.7 | async-start | bytes 4866048 | tf_op jit(solution)/shard_map/reduce_scatter | solution.py:778
  155.8 17.9 %copy-start.1 = (bf16[2,1,256,768]{3,2,1,0:T(8,128)(2,1)S(1)}, bf16[2,1,256,768]{3,2,1,0:T(8,128)(2,1)}, u32[]{:S(2)}) copy-start(bf16[2,1,256,768]{3,2,1,0:T(8,128)(2,1)} %param.25) | copy-start | bytes 2359300
  180.0 1.7 copy-start.10
  186.5 378.3 %reduce-scatter.15.cloned.1.call-start = ((), (), s32[]{:S(2)}) async-start(), calls=%async_computation.8 | async-start | bytes 4866048 | tf_op jit(solution)/shard_map/reduce_scatter | solution.py:778
  193.6 6.1 %copy-start.6 = (f32[512,768]{1,0:T(8,128)S(1)}, f32[512,768]{1,0:T(8,128)}, u32[]{:S(2)}) copy-start(f32[512,768]{1,0:T(8,128)} %get-tuple-element.44) | copy-start | bytes 4718596
  193.6 6.1 %copy-start.9 = (bf16[512,3072]{1,0:T(8,128)(2,1)S(1)}, bf16[512,3072]{1,0:T(8,128)(2,1)}, u32[]{:S(2)}) copy-start(bf16[512,3072]{1,0:T(8,128)(2,1)} %get-tuple-element.124) | copy-start | bytes 9437188
  199.7 6.0 %copy-start.5 = (f32[512,768]{1,0:T(8,128)S(1)}, f32[512,768]{1,0:T(8,128)}, u32[]{:S(2)}) copy-start(f32[512,768]{1,0:T(8,128)} %get-tuple-element.49) | copy-start | bytes 4718596
  199.8 6.0 %copy-start.7 = (bf16[768,128]{1,0:T(8,128)(2,1)S(1)}, bf16[768,128]{1,0:T(8,128)(2,1)}, u32[]{:S(2)}) copy-start(bf16[768,128]{1,0:T(8,128)(2,1)} %get-tuple-element.51) | copy-start | bytes 589828
  205.8 2.4 copy-start.4
Sparse Core Ops, SparseCore 0:
  111.4 39.2 reduce-scatter.8
  156.2 80.5 reduce-scatter.16
  242.9 98.0 reduce-scatter.10
  346.3 106.0 reduce-scatter.12
  458.7 106.0 reduce-scatter.14
